TPU v7x, 1024 devices: a whole 4x8x16 slice. The times are simulated.
1024 devices in a mesh: dp: 16 (over y, core), fsdp: 16 (over z), mp: 4 (over x).
Axes of the slice: x: 4, y: 8, z: 16, core: 2. Of those that a mesh axis runs over, the one named last changes fastest.
Arguments:
- gradient: bfloat16 [16, 4, 16, 512, 256], P('dp', 'mp', None, 'fsdp'), may hold values from -6 to 6
- owner_table: int32 [8, 4, 16], P(None, 'mp'), may hold values from 0 to 15, each once within a row
- refresh: int32 [16, 4, 16], P('dp', 'mp', 'fsdp'), may hold values from 0 to 1, as said below
- statistics: float32 [16, 4, 16, 512, 512], P('dp', 'mp', 'fsdp'), may hold values from -1 to 5, as said below
- inv_roots: bfloat16 [16, 4, 16, 512, 512], P('dp', 'mp', 'fsdp'), may hold values from -1 to 3, as said below
Outputs:
- update: bfloat16 [16, 4, 16, 512, 256], P('dp', 'mp', None, 'fsdp')
- new_stats: float32 [16, 4, 16, 512, 512], P('dp', 'mp', 'fsdp')
Inputs may be any that keep to these rules, and one draw needn't show every extreme that they name: `owner_table`: for each block column, a permutation of the 16 block rows onto the owner slots. `refresh`: for each side, block column group and slot, exactly one of the 4 mp indices is 1. `statistics`: every matrix is symmetric with a positive diagonal. `inv_roots`: every matrix is symmetric with a positive diagonal.
All inputs are finite; a program needn't handle non-finite values. Where the computation divides by a largest or mean magnitude, that divisor is 1e-20 or more.
Results may differ from a plain program's by a relative error of at most 0.0059.
Values may be sent and summed in bfloat16 or wider, within the bound.
No kernel may reach another device: no remote copies, remote signals or barrier semaphores. Data moves between devices by JAX's collectives and lax.ppermute only.
A program may use at most 32 MiB of HBM per device.

v0:
```python
import jax
import jax.numpy as jnp
from jax import lax
from jax.sharding import PartitionSpec as P

ITERS = 2


stat_decay = 0.9


def from_partner(value, axis, apart):
    mask = 2**apart
    pairs = [(source, source ^ mask) for source in range(lax.axis_size(axis))]
    return lax.ppermute(value, axis, pairs)


def batch_matmul(left_mat, right_mat):
    return jnp.einsum("...ij,...jk->...ik", left_mat, right_mat, preferred_element_type=jnp.float32)


def newton_batch(matrix):
    identity = jnp.eye(matrix.shape[-1], dtype=jnp.float32)
    row_bound = jnp.max(jnp.sum(jnp.abs(matrix), axis=-1), axis=-1)[..., None, None]
    scaling = 2.5 / row_bound
    iterate = scaling * matrix
    root_est = jnp.zeros_like(matrix)
    for newton_turn in range(ITERS):
        step_mat = ((5.0 * identity - iterate) * 0.25).astype(jnp.bfloat16)
        if newton_turn == 0:
            root_est = scaling**0.25 * lax.optimization_barrier(step_mat).astype(jnp.float32)
        else:
            root_est = batch_matmul(root_est.astype(jnp.bfloat16), step_mat)
        if newton_turn + 1 < ITERS:
            square = batch_matmul(step_mat, step_mat).astype(jnp.bfloat16)
            fourth = batch_matmul(square, square).astype(jnp.bfloat16)
            iterate = batch_matmul(fourth, iterate.astype(jnp.bfloat16))
    return root_est.astype(jnp.bfloat16)


def shards(gradient, owner_table, refresh, statistics, inv_roots):
    block_size = statistics.shape[-1]
    half_cols = block_size // 2
    local_cols = refresh.shape[0]
    dp_count = lax.axis_size("dp")
    half_group = dp_count // 2
    dp_index = lax.axis_index("dp")
    which_side = dp_index // half_group
    start_col = dp_index % half_group * local_cols
    slot_order = lax.dynamic_slice_in_dim(owner_table[:, 0, :], start_col, local_cols, 0)
    grad_bf = gradient[:, 0]
    inverse = jnp.argsort(slot_order, axis=1)
    outgoing = jnp.take_along_axis(grad_bf, inverse[:, :, None, None], axis=1)
    received = lax.all_to_all(outgoing, "fsdp", split_axis=1, concat_axis=2, tiled=True)
    own_stats = statistics[:, 0]
    own_roots = inv_roots[:, 0]
    own_mask = refresh[:, 0]
    marked_flag = own_mask[:, :, None, None] == 1
    fresh_roots = newton_batch(own_stats)
    new_root = jnp.where(marked_flag, fresh_roots, own_roots)
    swap_bit = dp_count.bit_length() - 2
    other_half, other_root = from_partner((received, new_root), "dp", swap_bit)
    is_left = which_side == 0
    left_first = jnp.concatenate([received, other_half], axis=3)
    right_first = jnp.concatenate([other_half, received], axis=3)
    full_block = jnp.where(is_left, left_first, right_first)
    gram_input = jnp.where(is_left, full_block, jnp.swapaxes(full_block, 2, 3))
    gram = jnp.einsum("abij,abkj->abik", gram_input, gram_input, preferred_element_type=jnp.float32)
    new_stat = stat_decay * own_stats + (1.0 - stat_decay) / block_size * gram
    left_root = jnp.where(is_left, new_root, other_root)
    right_root = jnp.where(is_left, other_root, new_root)
    partial_value = batch_matmul(left_root, full_block).astype(jnp.bfloat16)
    right_cols = lax.dynamic_slice_in_dim(right_root, which_side * half_cols, half_cols, 3)
    result_half = batch_matmul(partial_value, right_cols).astype(jnp.bfloat16)
    returned = lax.all_to_all(result_half, "fsdp", split_axis=2, concat_axis=1, tiled=True)
    update = jnp.take_along_axis(returned, slot_order[:, :, None, None], axis=1)
    return (update[:, None], new_stat[:, None])


def solution(mesh):
    return jax.shard_map(
        shards,
        mesh=mesh,
        in_specs=(
            P("dp", "mp", None, "fsdp", None),
            P(None, "mp", None),
            P("dp", "mp", "fsdp"),
            P("dp", "mp", "fsdp", None, None),
            P("dp", "mp", "fsdp", None, None),
        ),
        out_specs=(P("dp", "mp", None, "fsdp", None), P("dp", "mp", "fsdp", None, None)),
        check_vma=False,
    )
```

profile of v0, /device:TPU:22, one launch (start us, length us, event | category | flops | bytes accessed | tf_op | source)
XLA Modules:
  0.0 107.9 jit_solution(2765770105940609460)
XLA Ops:
  0.7 0.8 fusion.72
  1.5 0.7 sort.17
  2.3 0.7 fusion.59
  3.0 0.6 gather_fusion
  3.6 0.8 bitcast_select_fusion.3
  4.4 18.9 %all-to-all-start = ((bf16[1,16,32,256]{3,2,0,1:T(8,128)(2,1)}), bf16[1,16,32,256]{3,2,0,1:T(8,128)(2,1)S(1)}, u32[]{:S(2)}, u32[]{:S(2)}) async-start(bf16[1,16,32,256]{3,2,0,1:T(8,128)(2,1)} %bitcast_select_fusion.3), calls=%async_computation | async-start | bytes 524288 | tf_op jit(solution)/shard_map/all_to_all | solution.py:54
  23.5 0.6 reduce_max.9
  25.6 1.1 %convolution_convert_fusion.2 = bf16[512,512]{1,0:T(8,128)(2,1)S(1)} fusion(f32[1,1,1,512,512]{4,3,2,1,0:T(8,128)S(1)} %copy-done.1, f32[]{:T(128)S(6)} %div.15), kind=kOutput, calls=%fused_computation.10 | convolution fusion | flops 538968064 | bytes 1572868 | tf_op jit(solution)/shard_map/...ij,...jk->...ik/dot_general | solution.py:19
  26.7 1.6 %fusion.5 = bf16[1,1,512,512]{3,2,1,0:T(8,128)(2,1)} fusion(bf16[512,512]{1,0:T(8,128)(2,1)S(1)} %convolution_convert_fusion.2, f32[1,1,1,512,512]{4,3,2,1,0:T(8,128)S(1)} %copy-done.1, bf16[1,1,512,512]{3,2,1,0:T(8,128)(2,1)S(1)} %fusion.10, bf16[1,1,1,512,512]{4,3,2,1,0:T(8,128)(2,1)S(1)} %copy-done.2, f32[]{:T(128)S(6)} %div.15, f32[]{:T(128)S(6)} %pow.4, ...), kind=kOutput, calls=%fused_computation.13 | convolution fusion | flops 540016640 | bytes 3145737 | tf_op jit(solution)/shard_map/...ij,...jk->...ik/dot_general | solution.py:19
  28.3 5.9 %collective-permute-start = (bf16[1,1,512,512]{3,2,1,0:T(8,128)(2,1)}, bf16[1,1,512,512]{3,2,1,0:T(8,128)(2,1)}, u32[]{:S(2)}, u32[]{:S(2)}) collective-permute-start(bf16[1,1,512,512]{3,2,1,0:T(8,128)(2,1)} %fusion.5), channel_id=1, source_target_pairs={{0,512},{64,576},{128,640},{192,704},{256,768},{320,832},{384,896}... | collective-permute-start | bytes 1572872 | tf_op jit(solution)/shard_map/ppermute | solution.py:15
  34.3 7.4 %all-to-all-done = bf16[1,16,32,256]{3,2,0,1:T(8,128)(2,1)S(1)} async-done(((bf16[1,16,32,256]{3,2,0,1:T(8,128)(2,1)}), bf16[1,16,32,256]{3,2,0,1:T(8,128)(2,1)S(1)}, u32[]{:S(2)}, u32[]{:S(2)}) %all-to-all-start) | async-done | bytes 262176 | tf_op jit(solution)/shard_map/all_to_all | solution.py:54
  41.8 5.9 %collective-permute-start.1 = (bf16[1,1,512,256]{2,3,1,0:T(8,128)(2,1)S(1)}, bf16[1,1,512,256]{2,3,1,0:T(8,128)(2,1)S(1)}, u32[]{:S(2)}, u32[]{:S(2)}) collective-permute-start(bf16[1,1,512,256]{2,3,1,0:T(8,128)(2,1)S(1)} %copy.37), channel_id=1, source_target_pairs={{0,512},{64,576},{128,640},{192,704},{256,768},{320,832},{384,896}... | collective-permute-start | bytes 786440 | tf_op jit(solution)/shard_map/ppermute | solution.py:15
  47.9 17.0 %collective-permute-done = bf16[1,1,512,512]{3,2,1,0:T(8,128)(2,1)} collective-permute-done((bf16[1,1,512,512]{3,2,1,0:T(8,128)(2,1)}, bf16[1,1,512,512]{3,2,1,0:T(8,128)(2,1)}, u32[]{:S(2)}, u32[]{:S(2)}) %collective-permute-start) | collective-permute-done | bytes 524320 | tf_op jit(solution)/shard_map/ppermute | solution.py:15
  64.9 5.4 %collective-permute-done.1 = bf16[1,1,512,256]{2,3,1,0:T(8,128)(2,1)S(1)} collective-permute-done((bf16[1,1,512,256]{2,3,1,0:T(8,128)(2,1)S(1)}, bf16[1,1,512,256]{2,3,1,0:T(8,128)(2,1)S(1)}, u32[]{:S(2)}, u32[]{:S(2)}) %collective-permute-start.1) | collective-permute-done | bytes 262176 | tf_op jit(solution)/shard_map/ppermute | solution.py:15
  70.3 1.9 %fusion.8 = bf16[1,1,512,256]{3,2,1,0:T(8,128)(2,1)S(1)} fusion(bf16[512,256]{0,1:T(8,128)(2,1)S(1)} %bitcast.91, bf16[512,256]{0,1:T(8,128)(2,1)S(1)} %copy.38, bf16[1,1,512,512]{3,2,1,0:T(8,128)(2,1)} %fusion.5, bf16[1,1,512,512]{3,2,1,0:T(8,128)(2,1)} %collective-permute-done, pred[]{:T(512)S(6)} %eq.33, s32[]{:T(128)S(6)} %select_n.81), kind=kOutput, calls=%fused_computation.16 | convolution fusion | flops 405798912 | bytes 2361344 | tf_op jit(solution)/shard_map/...ij,...jk->...ik/dot_general | solution.py:19
  72.7 0.5 broadcast.222
  73.2 2.2 %reduce.5 = bf16[512,256]{1,0:T(8,128)(2,1)S(1)} reduce(bf16[512,1,1,256]{3,2,1,0:T(2,128)(2,1)S(1)} %bitcast.89, bf16[]{:T(256)} %broadcast.222), dimensions={1,2}, to_apply=%bitcast.84.reduce_sub_computation | reduce | bytes 524290
  75.4 0.8 reshape.291
  76.2 11.7 %all-to-all-start.1 = ((bf16[16,2,4096]{2,1,0:T(2,128)(2,1)}), bf16[16,2,4096]{2,1,0:T(2,128)(2,1)S(1)}, u32[]{:S(2)}, u32[]{:S(2)}) async-start(bf16[16,2,4096]{2,1,0:T(2,128)(2,1)} %reshape.291), calls=%async_computation.1 | async-start | bytes 524288 | tf_op jit(solution)/shard_map/all_to_all | solution.py:75
  87.9 0.7 and_bitcast_fusion
  89.0 1.5 %fusion.1 = f32[1,1,1,512,512]{4,3,2,1,0:T(8,128)} fusion(f32[1,1,1,512,512]{4,3,2,1,0:T(8,128)S(1)} %copy-done.1, bf16[1,1,512,512]{3,2,1,0:T(8,128)(2,1)S(1)} %copy.44, pred[]{:T(512)S(6)} %eq.33, bf16[1,1,512,256]{2,3,1,0:T(8,128)(2,1)S(1)} %collective-permute-done.1, bf16[1,1,512,256]{2,3,1,0:T(8,128)(2,1)S(1)} %copy.37), kind=kOutput, calls=%fused_computation.4 | convolution fusion | flops 271843328 | bytes 3145729 | tf_op jit(solution)/shard_map/abij,abkj->abik/dot_general | solution.py:68
  90.5 15.7 %all-to-all-done.1 = bf16[16,2,4096]{2,1,0:T(2,128)(2,1)S(1)} async-done(((bf16[16,2,4096]{2,1,0:T(2,128)(2,1)}), bf16[16,2,4096]{2,1,0:T(2,128)(2,1)S(1)}, u32[]{:S(2)}, u32[]{:S(2)}) %all-to-all-start.1) | async-done | bytes 262176 | tf_op jit(solution)/shard_map/all_to_all | solution.py:75
  106.5 0.6 gather_fusion.1
  107.1 0.8 fusion.56
  (21 shorter events, 2.0 us)
Async XLA Ops:
  0.6 2.4 %copy-start = (bf16[1,1,16,32,256]{4,3,2,1,0:T(8,128)(2,1)S(1)}, bf16[1,1,16,32,256]{4,3,2,1,0:T(8,128)(2,1)}, u32[]{:S(2)}) copy-start(bf16[1,1,16,32,256]{4,3,2,1,0:T(8,128)(2,1)} %param.7) | copy-start | bytes 786436
  0.6 22.6 %copy-start.1 = (f32[1,1,1,512,512]{4,3,2,1,0:T(8,128)S(1)}, f32[1,1,1,512,512]{4,3,2,1,0:T(8,128)}, u32[]{:S(2)}) copy-start(f32[1,1,1,512,512]{4,3,2,1,0:T(8,128)} %param.10) | copy-start | bytes 3145732
  4.4 37.2 %all-to-all-start = ((bf16[1,16,32,256]{3,2,0,1:T(8,128)(2,1)}), bf16[1,16,32,256]{3,2,0,1:T(8,128)(2,1)S(1)}, u32[]{:S(2)}, u32[]{:S(2)}) async-start(bf16[1,16,32,256]{3,2,0,1:T(8,128)(2,1)} %bitcast_select_fusion.3), calls=%async_computation | async-start | bytes 524288 | tf_op jit(solution)/shard_map/all_to_all | solution.py:54
  25.6 1.1 %copy-start.2 = (bf16[1,1,1,512,512]{4,3,2,1,0:T(8,128)(2,1)S(1)}, bf16[1,1,1,512,512]{4,3,2,1,0:T(8,128)(2,1)}, u32[]{:S(2)}) copy-start(bf16[1,1,1,512,512]{4,3,2,1,0:T(8,128)(2,1)} %param.11) | copy-start | bytes 1572868
  28.3 36.6 %collective-permute-start = (bf16[1,1,512,512]{3,2,1,0:T(8,128)(2,1)}, bf16[1,1,512,512]{3,2,1,0:T(8,128)(2,1)}, u32[]{:S(2)}, u32[]{:S(2)}) collective-permute-start(bf16[1,1,512,512]{3,2,1,0:T(8,128)(2,1)} %fusion.5), channel_id=1, source_target_pairs={{0,512},{64,576},{128,640},{192,704},{256,768},{320,832},{384,896}... | collective-permute-start | bytes 1572872 | tf_op jit(solution)/shard_map/ppermute | solution.py:15
  41.8 28.5 %collective-permute-start.1 = (bf16[1,1,512,256]{2,3,1,0:T(8,128)(2,1)S(1)}, bf16[1,1,512,256]{2,3,1,0:T(8,128)(2,1)S(1)}, u32[]{:S(2)}, u32[]{:S(2)}) collective-permute-start(bf16[1,1,512,256]{2,3,1,0:T(8,128)(2,1)S(1)} %copy.37), channel_id=1, source_target_pairs={{0,512},{64,576},{128,640},{192,704},{256,768},{320,832},{384,896}... | collective-permute-start | bytes 786440 | tf_op jit(solution)/shard_map/ppermute | solution.py:15
  76.2 30.0 %all-to-all-start.1 = ((bf16[16,2,4096]{2,1,0:T(2,128)(2,1)}), bf16[16,2,4096]{2,1,0:T(2,128)(2,1)S(1)}, u32[]{:S(2)}, u32[]{:S(2)}) async-start(bf16[16,2,4096]{2,1,0:T(2,128)(2,1)} %reshape.291), calls=%async_computation.1 | async-start | bytes 524288 | tf_op jit(solution)/shard_map/all_to_all | solution.py:75
where the time goes:
time: 108 us
  waiting for transfers between devices  45.5 us (42%)
  starting transfers between devices  42.4 us (39%)
  other arithmetic  7.1 us (7%)
  matrix products  6.13 us (6%)
  local copies, waits for them, and re-layouts  4.48 us (4%)
  between operations  2.25 us (2%)
    ppermute x2, waiting for transfers between devices, from_partner(): return lax.ppermute(value, axis, pairs)  22.4 us
    all_to_all x1, starting transfers between devices, shards(): lax.all_to_all(outgoing, 'fsdp', split_axis=1, concat_axis=2, tiled=True)  18.9 us
    all_to_all x1, waiting for transfers between devices, shards(): lax.all_to_all(result_half, 'fsdp', split_axis=2, concat_axis=1, tiled=True)  15.7 us
    ppermute x2, starting transfers between devices, from_partner(): return lax.ppermute(value, axis, pairs)  11.9 us
    all_to_all x1, starting transfers between devices, shards(): lax.all_to_all(result_half, 'fsdp', split_axis=2, concat_axis=1, tiled=True)  11.7 us
    all_to_all x1, waiting for transfers between devices, shards(): lax.all_to_all(outgoing, 'fsdp', split_axis=1, concat_axis=2, tiled=True)  7.36 us
    dot_general x3, matrix products, batch_matmul(): jnp.einsum('...ij,...jk->...ik', left_mat, right_mat, preferred_element_t...  4.62 us
    unnamed x1, other arithmetic  2.21 us
  transfers between devices with their start and end apart: 4, of which 4 were waited for; matrix products, arithmetic and copies ran while one was open for 6% of the time, Pallas kernels for 0%

commit v1 on v0

v1 whole, which is shorter than its diff:
```python
import functools

import jax
import jax.numpy as jnp
from jax import lax
from jax.experimental import pallas as pl
from jax.experimental.pallas import tpu as pltpu
from jax.sharding import PartitionSpec as P

ITERS = 2
STAT_DECAY = 0.9
MIB = 1024 * 1024

VMEM = pl.BlockSpec(memory_space=pltpu.VMEM)
SMEM = pl.BlockSpec(memory_space=pltpu.SMEM)
ANY = pl.BlockSpec(memory_space=pl.ANY)


def dot(left, right, contract=((1,), (0,))):
    return lax.dot_general(left, right, (contract, ((), ())), preferred_element_type=jnp.float32)


def flip(block):
    return block.astype(jnp.float32).T.astype(block.dtype)


def to_slots_kernel(groups, table_ref, grad_ref, out_ref, sems):
    group = lax.rem(lax.axis_index("dp"), groups)
    copies = []
    for r in range(grad_ref.shape[0]):
        slot = table_ref[group, 0, r]
        copies.append(pltpu.make_async_copy(grad_ref.at[r], out_ref.at[slot], sems.at[r]))
        copies[-1].start()
    for copy in copies:
        copy.wait()


def from_slots_kernel(groups, table_ref, got_ref, out_ref, sems):
    group = lax.rem(lax.axis_index("dp"), groups)
    copies = []
    for r in range(out_ref.shape[0]):
        slot = table_ref[group, 0, r]
        copies.append(pltpu.make_async_copy(got_ref.at[slot], out_ref.at[r], sems.at[r]))
        copies[-1].start()
    for copy in copies:
        copy.wait()


def move_blocks(body, groups, table, blocks):
    return pl.pallas_call(
        functools.partial(body, groups),
        out_shape=jax.ShapeDtypeStruct(blocks.shape, blocks.dtype),
        in_specs=[SMEM, ANY],
        out_specs=ANY,
        scratch_shapes=[pltpu.SemaphoreType.DMA((blocks.shape[0],))],
        compiler_params=pltpu.CompilerParams(vmem_limit_bytes=MIB),
        cost_estimate=pl.CostEstimate(flops=0, bytes_accessed=2 * blocks.size * 2, transcendentals=0),
    )(table, blocks)


def root_kernel(flag_ref, stat_ref, old_ref, root_ref, pack_ref):
    order = stat_ref.shape[0]
    half = order // 2

    @pl.when(flag_ref[0, 0, 0] == 1)
    def _():
        matrix = stat_ref[...]
        rows = lax.broadcasted_iota(jnp.int32, (order, order), 0)
        cols = lax.broadcasted_iota(jnp.int32, (order, order), 1)
        on_diag = rows == cols
        bound = jnp.max(jnp.sum(jnp.abs(matrix), axis=0, keepdims=True), axis=1, keepdims=True)
        scaling = 2.5 / bound
        iterate = scaling * matrix
        root = None
        for turn in range(ITERS):
            step = (jnp.where(on_diag, 5.0 - iterate, -iterate) * 0.25).astype(jnp.bfloat16)
            if turn == 0:
                root = jnp.sqrt(jnp.sqrt(scaling)) * step.astype(jnp.float32)
            else:
                root = dot(root.astype(jnp.bfloat16), step)
            if turn + 1 < ITERS:
                square = dot(step, step).astype(jnp.bfloat16)
                fourth = dot(square, square).astype(jnp.bfloat16)
                iterate = dot(fourth, iterate.astype(jnp.bfloat16))
        root_ref[...] = root.astype(jnp.bfloat16)

    @pl.when(flag_ref[0, 0, 0] != 1)
    def _():
        root_ref[...] = old_ref[...]

    rows = lax.broadcasted_iota(jnp.int32, (half, half), 0)
    cols = lax.broadcasted_iota(jnp.int32, (half, half), 1)
    first = root_ref[0:half, 0:half].astype(jnp.float32)
    second = root_ref[half:order, half:order].astype(jnp.float32)
    pack_ref[0:half, :] = jnp.where(rows <= cols, first, second).astype(jnp.bfloat16)
    pack_ref[half:order, :] = root_ref[half:order, 0:half]
    diagonal = jnp.sum(jnp.where(rows == cols, second, 0.0), axis=0, keepdims=True)
    pack_ref[order : order + 16, :] = jnp.broadcast_to(diagonal, (16, half)).astype(jnp.bfloat16)


def fresh_and_packed(flag, stat, old):
    order = stat.shape[0]
    return pl.pallas_call(
        root_kernel,
        out_shape=(
            jax.ShapeDtypeStruct((order, order), jnp.bfloat16),
            jax.ShapeDtypeStruct((order + 16, order // 2), jnp.bfloat16),
        ),
        in_specs=[SMEM, VMEM, VMEM],
        out_specs=(VMEM, VMEM),
        compiler_params=pltpu.CompilerParams(vmem_limit_bytes=24 * MIB),
        cost_estimate=pl.CostEstimate(flops=8 * order**3, bytes_accessed=9 * order**2, transcendentals=0),
    )(flag, stat, old)


def own_kernel(half_group, root_ref, pack_ref, own_ref, left_ref, right_ref, partial_ref):
    order = root_ref.shape[0]
    half = order // 2
    side = lax.axis_index("dp") // half_group
    rows = lax.broadcasted_iota(jnp.int32, (half, half), 0)
    cols = lax.broadcasted_iota(jnp.int32, (half, half), 1)
    tri = pack_ref[0:half, :].astype(jnp.float32)
    tri_flipped = tri.T
    first = jnp.where(rows <= cols, tri, tri_flipped).astype(jnp.bfloat16)

    @pl.when(side == 0)
    def _():
        left_ref[...] = root_ref[...]
        right_ref[0:half, :] = first
        right_ref[half:order, :] = pack_ref[half:order, :]

    @pl.when(side != 0)
    def _():
        right_ref[...] = root_ref[:, half:order]
        diagonal = pack_ref[order : order + 16, :].astype(jnp.float32)[0:1, :]
        second = jnp.where(rows > cols, tri, jnp.where(rows == cols, diagonal, tri_flipped))
        left_ref[0:half, 0:half] = first
        left_ref[half:order, half:order] = second.astype(jnp.bfloat16)
        left_ref[half:order, 0:half] = pack_ref[half:order, :]
        left_ref[0:half, half:order] = flip(pack_ref[half:order, :])

    partial_ref[...] = dot(left_ref[...], own_ref[...]).astype(jnp.bfloat16)


def own_part(half_group, root, pack, own):
    order = root.shape[0]
    half = order // 2
    return pl.pallas_call(
        functools.partial(own_kernel, half_group),
        out_shape=(
            jax.ShapeDtypeStruct((order, order), jnp.bfloat16),
            jax.ShapeDtypeStruct((order, half), jnp.bfloat16),
            jax.ShapeDtypeStruct((order, half), jnp.bfloat16),
        ),
        in_specs=[VMEM] * 3,
        out_specs=(VMEM,) * 3,
        compiler_params=pltpu.CompilerParams(vmem_limit_bytes=16 * MIB),
        cost_estimate=pl.CostEstimate(flops=order**3, bytes_accessed=6 * order**2, transcendentals=0),
    )(root, pack, own)


def result_kernel(half_group, left_ref, right_ref, partial_ref, other_ref, out_ref):
    order = left_ref.shape[0]
    half = order // 2
    side = lax.axis_index("dp") // half_group
    mine = pl.ds(pl.multiple_of(side * half, half), half)
    theirs = pl.ds(pl.multiple_of((1 - side) * half, half), half)
    other_partial = dot(left_ref[...], other_ref[...]).astype(jnp.bfloat16)
    total = dot(partial_ref[...], right_ref[mine, :]) + dot(other_partial, right_ref[theirs, :])
    out_ref[...] = total.astype(jnp.bfloat16)


def result_half(half_group, left, right, partial, other):
    order = left.shape[0]
    return pl.pallas_call(
        functools.partial(result_kernel, half_group),
        out_shape=jax.ShapeDtypeStruct(other.shape, jnp.bfloat16),
        in_specs=[VMEM] * 4,
        out_specs=VMEM,
        compiler_params=pltpu.CompilerParams(vmem_limit_bytes=16 * MIB),
        cost_estimate=pl.CostEstimate(flops=2 * order**3, bytes_accessed=6 * order**2, transcendentals=0),
    )(left, right, partial, other)


def stats_kernel(half_group, stat_ref, own_ref, other_ref, out_ref):
    order = stat_ref.shape[0]
    half = order // 2
    side = lax.axis_index("dp") // half_group
    factor = (1.0 - STAT_DECAY) / order

    @pl.when(side == 0)
    def _():
        own, other = own_ref[...], other_ref[...]
        gram = dot(own, own, ((1,), (1,))) + dot(other, other, ((1,), (1,)))
        out_ref[...] = STAT_DECAY * stat_ref[...] + factor * gram

    @pl.when(side != 0)
    def _():
        halves = (other_ref[...], own_ref[...])
        for i in range(2):
            lines = slice(i * half, (i + 1) * half)
            turned = flip(halves[i])
            for j in range(2):
                columns = slice(j * half, (j + 1) * half)
                gram = dot(turned, halves[j])
                out_ref[lines, columns] = STAT_DECAY * stat_ref[lines, columns] + factor * gram


def updated_stats(half_group, stat, own, other):
    order = stat.shape[0]
    return pl.pallas_call(
        functools.partial(stats_kernel, half_group),
        out_shape=jax.ShapeDtypeStruct(stat.shape, jnp.float32),
        in_specs=[VMEM] * 3,
        out_specs=VMEM,
        compiler_params=pltpu.CompilerParams(vmem_limit_bytes=16 * MIB),
        cost_estimate=pl.CostEstimate(flops=2 * order**3, bytes_accessed=10 * order**2, transcendentals=0),
    )(stat, own, other)


def shards(gradient, owner_table, refresh, statistics, inv_roots):
    order = statistics.shape[-1]
    half = order // 2
    dp_count = lax.axis_size("dp")
    half_group = dp_count // 2
    swap = [(source, (source + half_group) % dp_count) for source in range(dp_count)]
    stat = statistics[0, 0, 0]
    outgoing = move_blocks(to_slots_kernel, half_group, owner_table, gradient[0, 0])
    received = lax.all_to_all(outgoing, "fsdp", split_axis=0, concat_axis=0, tiled=True)
    own = received.reshape(order, half)
    root, pack = fresh_and_packed(refresh, stat, inv_roots[0, 0, 0])
    other_pack = lax.ppermute(pack, "dp", swap)
    own, pack = lax.optimization_barrier((own, pack))
    other = lax.ppermute(own, "dp", swap)
    left, right, partial = own_part(half_group, root, other_pack, own)
    result = result_half(half_group, left, right, partial, other)
    result, own, other = lax.optimization_barrier((result, own, other))
    returned = lax.all_to_all(result.reshape(outgoing.shape), "fsdp", split_axis=0, concat_axis=0, tiled=True)
    new_stat = updated_stats(half_group, stat, own, other)
    update = move_blocks(from_slots_kernel, half_group, owner_table, returned)
    return update[None, None], new_stat[None, None, None]


def solution(mesh):
    return jax.shard_map(
        shards,
        mesh=mesh,
        in_specs=(
            P("dp", "mp", None, "fsdp", None),
            P(None, "mp", None),
            P("dp", "mp", "fsdp"),
            P("dp", "mp", "fsdp", None, None),
            P("dp", "mp", "fsdp", None, None),
        ),
        out_specs=(P("dp", "mp", None, "fsdp", None), P("dp", "mp", "fsdp", None, None)),
        check_vma=False,
    )
```

time: 108 us -> 92.6 us (0.86)
  the two profiles are of different devices: /device:TPU:22 before, /device:TPU:6 now
where the time goes in v1:
time: 92.6 us; the launch traced here: 92.2 us
  starting transfers between devices  49.3 us (53%)
  waiting for transfers between devices  32.5 us (35%)
  Pallas kernels  6.27 us (7%)
  local copies, waits for them, and re-layouts  2.76 us (3%)
  between operations  1.38 us (1%)
    all_to_all x1, starting transfers between devices, shards(): lax.all_to_all(outgoing, 'fsdp', split_axis=0, concat_axis=0, tiled=True)  18.9 us
    all_to_all x1, waiting for transfers between devices, shards(): lax.all_to_all(result.reshape(outgoing.shape), 'fsdp', split_axis=0, conc...  16.9 us
    all_to_all x1, starting transfers between devices, shards(): lax.all_to_all(result.reshape(outgoing.shape), 'fsdp', split_axis=0, conc...  15 us
    all_to_all x1, waiting for transfers between devices, shards(): lax.all_to_all(outgoing, 'fsdp', split_axis=0, concat_axis=0, tiled=True)  8.83 us
    ppermute x1, starting transfers between devices, shards(): other_pack = lax.ppermute(pack, 'dp', swap)  7.73 us
    ppermute x1, starting transfers between devices, shards(): other = lax.ppermute(own, 'dp', swap)  7.72 us
    ppermute x1, waiting for transfers between devices, shards(): other = lax.ppermute(own, 'dp', swap)  6.71 us
    pallas_call x2, Pallas kernels, move_blocks(): pl.pallas_call(functools.partial(body, groups), out_shape=jax.ShapeDtypeS...  2.88 us
  transfers between devices with their start and end apart: 4, of which 3 were waited for; matrix products, arithmetic and copies ran while one was open for 0% of the time, Pallas kernels for 2%

profile of v1, /device:TPU:6, one launch (start us, length us, event | category | flops | bytes accessed | tf_op | source)
XLA Modules:
  0.0 92.2 jit_solution(11168777738387473364)
XLA Ops:
  0.6 0.0 copy-start
  0.6 0.0 copy-start.1
  0.6 1.0 %copy-done.1 = bf16[1,1,16,32,256]{4,3,2,1,0:T(8,128)(2,1)S(1)} copy-done((bf16[1,1,16,32,256]{4,3,2,1,0:T(8,128)(2,1)S(1)}, bf16[1,1,16,32,256]{4,3,2,1,0:T(8,128)(2,1)}, u32[]{:S(2)}) %copy-start.1) | copy-done | bytes 262168
  1.7 0.0 copy-start.2
  1.7 0.7 copy-done.2
  2.4 1.4 %shard_map.69 = bf16[16,32,256]{2,1,0:T(8,128)(2,1)} custom-call(s32[8,1,16]{2,1,0:T(1,128)S(1)} %copy-done.2, bf16[16,32,256]{2,1,0:T(8,128)(2,1)S(1)} %bitcast.12), custom_call_target="tpu_custom_call" | custom-call | bytes 524288 | tf_op jit(solution)/shard_map/pallas_call | solution.py:50
  3.8 18.9 %all-to-all-start = ((bf16[16,32,256]{2,1,0:T(8,128)(2,1)}), bf16[16,32,256]{2,1,0:T(8,128)(2,1)S(1)}, u32[]{:S(2)}, u32[]{:S(2)}) async-start(bf16[16,32,256]{2,1,0:T(8,128)(2,1)} %shard_map.69), calls=%async_computation | async-start | bytes 524288 | tf_op jit(solution)/shard_map/all_to_all | solution.py:229
  23.3 0.0 copy-done
  23.4 0.0 copy-start.4
  23.4 1.0 %copy-done.4 = bf16[1,1,1,512,512]{4,3,2,1,0:T(8,128)(2,1)S(1)} copy-done((bf16[1,1,1,512,512]{4,3,2,1,0:T(8,128)(2,1)S(1)}, bf16[1,1,1,512,512]{4,3,2,1,0:T(8,128)(2,1)}, u32[]{:S(2)}) %copy-start.4) | copy-done | bytes 524312
  24.4 0.1 shard_map.68
  24.5 7.7 %collective-permute-start = (bf16[528,256]{1,0:T(8,128)(2,1)S(1)}, bf16[528,256]{1,0:T(8,128)(2,1)S(1)}, u32[]{:S(2)}, u32[]{:S(2)}) collective-permute-start(bf16[528,256]{1,0:T(8,128)(2,1)S(1)} %get-tuple-element.12), channel_id=1, source_target_pairs={{0,512},{64,576},{128,640},{192,704},{256,768},{320,832},{384,896}... | collective-permute-start | bytes 811016 | tf_op jit(solution)/shard_map/ppermute | solution.py:232
  32.2 8.8 %all-to-all-done = bf16[16,32,256]{2,1,0:T(8,128)(2,1)S(1)} async-done(((bf16[16,32,256]{2,1,0:T(8,128)(2,1)}), bf16[16,32,256]{2,1,0:T(8,128)(2,1)S(1)}, u32[]{:S(2)}, u32[]{:S(2)}) %all-to-all-start) | async-done | bytes 262176 | tf_op jit(solution)/shard_map/all_to_all | solution.py:229
  41.1 7.7 %collective-permute-start.1 = (bf16[512,256]{1,0:T(8,128)(2,1)S(1)}, bf16[512,256]{1,0:T(8,128)(2,1)S(1)}, u32[]{:S(2)}, u32[]{:S(2)}) collective-permute-start(bf16[512,256]{1,0:T(8,128)(2,1)S(1)} %bitcast.7), channel_id=1, source_target_pairs={{0,512},{64,576},{128,640},{192,704},{256,768},{320,832},{384,896}... | collective-permute-start | bytes 786440 | tf_op jit(solution)/shard_map/ppermute | solution.py:234
  48.8 0.0 collective-permute-done.pack_ref
  48.8 0.5 shard_map.70
  49.3 6.7 %collective-permute-done.1.other_ref = bf16[512,256]{1,0:T(8,128)(2,1)S(1)} collective-permute-done((bf16[512,256]{1,0:T(8,128)(2,1)S(1)}, bf16[512,256]{1,0:T(8,128)(2,1)S(1)}, u32[]{:S(2)}, u32[]{:S(2)}) %collective-permute-start.1) | collective-permute-done | bytes 262176 | tf_op jit(solution)/shard_map/ppermute | solution.py:234
  56.0 1.4 %shard_map.71 = bf16[512,256]{1,0:T(8,128)(2,1)} custom-call(bf16[512,512]{1,0:T(8,128)(2,1)S(1)} %get-tuple-element.14.left_ref, bf16[512,256]{1,0:T(8,128)(2,1)S(1)} %get-tuple-element.15.right_ref, bf16[512,256]{1,0:T(8,128)(2,1)S(1)} %get-tuple-element.16.partial_ref, bf16[512,256]{1,0:T(8,128)(2,1)S(1)} %collective-permute-done.1.other_ref), custom_call_target="tpu_custom_call" | custom-call | flops 268435456 | bytes 1572864 | tf_op jit(solution)/shard_map/pallas_call | solution.py:175
  57.3 15.0 %all-to-all-start.1 = ((bf16[16,32,256]{2,1,0:T(8,128)(2,1)}), bf16[16,32,256]{2,1,0:T(8,128)(2,1)S(1)}, u32[]{:S(2)}, u32[]{:S(2)}) async-start(bf16[16,32,256]{2,1,0:T(8,128)(2,1)} %bitcast.4), calls=%async_computation.1 | async-start | bytes 524288 | tf_op jit(solution)/shard_map/all_to_all | solution.py:238
  72.3 0.0 copy-start.3
  72.3 1.5 %shard_map.73 = f32[512,512]{1,0:T(8,128)} custom-call(f32[512,512]{1,0:T(8,128)S(1)} %bitcast.11, bf16[512,256]{1,0:T(8,128)(2,1)S(1)} %bitcast.9, bf16[512,256]{1,0:T(8,128)(2,1)S(1)} %collective-permute-done.1.other_ref), custom_call_target="tpu_custom_call" | custom-call | flops 268435456 | bytes 2621440 | tf_op jit(solution)/shard_map/pallas_call | solution.py:211
  73.8 16.9 %all-to-all-done.1.got_ref = bf16[16,32,256]{2,1,0:T(8,128)(2,1)S(1)} async-done(((bf16[16,32,256]{2,1,0:T(8,128)(2,1)}), bf16[16,32,256]{2,1,0:T(8,128)(2,1)S(1)}, u32[]{:S(2)}, u32[]{:S(2)}) %all-to-all-start.1) | async-done | bytes 262176 | tf_op jit(solution)/shard_map/all_to_all | solution.py:238
  90.7 0.0 copy-done.3
  90.7 1.4 %shard_map.72 = bf16[16,32,256]{2,1,0:T(8,128)(2,1)} custom-call(s32[8,1,16]{2,1,0:T(1,128)S(1)} %copy-done.3, bf16[16,32,256]{2,1,0:T(8,128)(2,1)S(1)} %all-to-all-done.1.got_ref), custom_call_target="tpu_custom_call" | custom-call | bytes 524288 | tf_op jit(solution)/shard_map/pallas_call | solution.py:50
Async XLA Ops:
  0.6 22.7 %copy-start = (f32[1,1,1,512,512]{4,3,2,1,0:T(8,128)S(1)}, f32[1,1,1,512,512]{4,3,2,1,0:T(8,128)}, u32[]{:S(2)}) copy-start(f32[1,1,1,512,512]{4,3,2,1,0:T(8,128)} %param.8) | copy-start | bytes 3145732
  0.6 1.0 %copy-start.1 = (bf16[1,1,16,32,256]{4,3,2,1,0:T(8,128)(2,1)S(1)}, bf16[1,1,16,32,256]{4,3,2,1,0:T(8,128)(2,1)}, u32[]{:S(2)}) copy-start(bf16[1,1,16,32,256]{4,3,2,1,0:T(8,128)(2,1)} %param.5) | copy-start | bytes 786436
  1.7 0.7 copy-start.2
  3.8 37.2 %all-to-all-start = ((bf16[16,32,256]{2,1,0:T(8,128)(2,1)}), bf16[16,32,256]{2,1,0:T(8,128)(2,1)S(1)}, u32[]{:S(2)}, u32[]{:S(2)}) async-start(bf16[16,32,256]{2,1,0:T(8,128)(2,1)} %shard_map.69), calls=%async_computation | async-start | bytes 524288 | tf_op jit(solution)/shard_map/all_to_all | solution.py:229
  23.4 1.0 %copy-start.4 = (bf16[1,1,1,512,512]{4,3,2,1,0:T(8,128)(2,1)S(1)}, bf16[1,1,1,512,512]{4,3,2,1,0:T(8,128)(2,1)}, u32[]{:S(2)}) copy-start(bf16[1,1,1,512,512]{4,3,2,1,0:T(8,128)(2,1)} %param.9) | copy-start | bytes 1572868
  24.5 24.3 %collective-permute-start = (bf16[528,256]{1,0:T(8,128)(2,1)S(1)}, bf16[528,256]{1,0:T(8,128)(2,1)S(1)}, u32[]{:S(2)}, u32[]{:S(2)}) collective-permute-start(bf16[528,256]{1,0:T(8,128)(2,1)S(1)} %get-tuple-element.12), channel_id=1, source_target_pairs={{0,512},{64,576},{128,640},{192,704},{256,768},{320,832},{384,896}... | collective-permute-start | bytes 811016 | tf_op jit(solution)/shard_map/ppermute | solution.py:232
  41.1 14.9 %collective-permute-start.1 = (bf16[512,256]{1,0:T(8,128)(2,1)S(1)}, bf16[512,256]{1,0:T(8,128)(2,1)S(1)}, u32[]{:S(2)}, u32[]{:S(2)}) collective-permute-start(bf16[512,256]{1,0:T(8,128)(2,1)S(1)} %bitcast.7), channel_id=1, source_target_pairs={{0,512},{64,576},{128,640},{192,704},{256,768},{320,832},{384,896}... | collective-permute-start | bytes 786440 | tf_op jit(solution)/shard_map/ppermute | solution.py:234
  57.3 33.4 %all-to-all-start.1 = ((bf16[16,32,256]{2,1,0:T(8,128)(2,1)}), bf16[16,32,256]{2,1,0:T(8,128)(2,1)S(1)}, u32[]{:S(2)}, u32[]{:S(2)}) async-start(bf16[16,32,256]{2,1,0:T(8,128)(2,1)} %bitcast.4), calls=%async_computation.1 | async-start | bytes 524288 | tf_op jit(solution)/shard_map/all_to_all | solution.py:238
  72.3 18.4 %copy-start.3 = (s32[8,1,16]{2,1,0:T(1,128)S(1)}, s32[8,1,16]{2,1,0:T(1,128)}, u32[]{:S(2)}) copy-start(s32[8,1,16]{2,1,0:T(1,128)} %table_ref.3) | copy-start | bytes 1540

commit v2 on v1

--- a/solution.py
+++ b/solution.py
@@ -13,7 +13,7 @@
 
 VMEM = pl.BlockSpec(memory_space=pltpu.VMEM)
 SMEM = pl.BlockSpec(memory_space=pltpu.SMEM)
-ANY = pl.BlockSpec(memory_space=pl.ANY)
+HBM = pl.BlockSpec(memory_space=pltpu.HBM)
 
 
 def dot(left, right, contract=((1,), (0,))):
@@ -24,15 +24,46 @@
     return block.astype(jnp.float32).T.astype(block.dtype)
 
 
-def to_slots_kernel(groups, table_ref, grad_ref, out_ref, sems):
+def load_kernel(groups, table_ref, grad_ref, stat_ref, old_ref, out_ref, stat_out, old_out, table_out, held, sems, move_sems):
+    copies = [
+        pltpu.make_async_copy(source, target, sems.at[i])
+        for i, (source, target) in enumerate(
+            ((table_ref, table_out), (grad_ref, held), (stat_ref, stat_out), (old_ref, old_out))
+        )
+    ]
+    for copy in copies:
+        copy.start()
     group = lax.rem(lax.axis_index("dp"), groups)
-    copies = []
-    for r in range(grad_ref.shape[0]):
-        slot = table_ref[group, 0, r]
-        copies.append(pltpu.make_async_copy(grad_ref.at[r], out_ref.at[slot], sems.at[r]))
-        copies[-1].start()
-    for copy in copies:
+    copies[0].wait()
+    copies[1].wait()
+    moves = []
+    for r in range(held.shape[0]):
+        moves.append(pltpu.make_async_copy(held.at[r], out_ref.at[table_out[group, 0, r]], move_sems.at[r]))
+        moves[-1].start()
+    for copy in copies[2:] + moves:
         copy.wait()
+
+
+def load(groups, table, grad, stat, old):
+    size = 2 * grad.size * 2 + 4 * stat.size + 2 * old.size
+    return pl.pallas_call(
+        functools.partial(load_kernel, groups),
+        out_shape=(
+            pltpu.HBM(grad.shape, grad.dtype),
+            pltpu.VMEM(stat.shape, stat.dtype),
+            pltpu.VMEM(old.shape, old.dtype),
+            pltpu.SMEM(table.shape, table.dtype),
+        ),
+        in_specs=[HBM] * 4,
+        out_specs=(HBM, VMEM, VMEM, SMEM),
+        scratch_shapes=[
+            pltpu.VMEM(grad.shape, grad.dtype),
+            pltpu.SemaphoreType.DMA((4,)),
+            pltpu.SemaphoreType.DMA((grad.shape[0],)),
+        ],
+        compiler_params=pltpu.CompilerParams(vmem_limit_bytes=4 * MIB),
+        cost_estimate=pl.CostEstimate(flops=0, bytes_accessed=size, transcendentals=0),
+    )(*(pltpu.with_memory_space_constraint(x, pltpu.HBM) for x in (table, grad, stat, old)))
 
 
 def from_slots_kernel(groups, table_ref, got_ref, out_ref, sems):
@@ -46,12 +77,12 @@
         copy.wait()
 
 
-def move_blocks(body, groups, table, blocks):
-    return pl.pallas_call(
-        functools.partial(body, groups),
+def from_slots(groups, table, blocks):
+    return pl.pallas_call(
+        functools.partial(from_slots_kernel, groups),
         out_shape=jax.ShapeDtypeStruct(blocks.shape, blocks.dtype),
-        in_specs=[SMEM, ANY],
-        out_specs=ANY,
+        in_specs=[SMEM, VMEM],
+        out_specs=HBM,
         scratch_shapes=[pltpu.SemaphoreType.DMA((blocks.shape[0],))],
         compiler_params=pltpu.CompilerParams(vmem_limit_bytes=MIB),
         cost_estimate=pl.CostEstimate(flops=0, bytes_accessed=2 * blocks.size * 2, transcendentals=0),
@@ -113,7 +144,7 @@
     )(flag, stat, old)
 
 
-def own_kernel(half_group, root_ref, pack_ref, own_ref, left_ref, right_ref, partial_ref):
+def own_kernel(half_group, root_ref, pack_ref, own_ref, left_ref, right_ref, total_ref):
     order = root_ref.shape[0]
     half = order // 2
     side = lax.axis_index("dp") // half_group
@@ -123,23 +154,26 @@
     tri_flipped = tri.T
     first = jnp.where(rows <= cols, tri, tri_flipped).astype(jnp.bfloat16)
 
+    def own_total(right_own):
+        partial = dot(left_ref[...], own_ref[...]).astype(jnp.bfloat16)
+        total_ref[...] = dot(partial, right_own)
+
     @pl.when(side == 0)
     def _():
         left_ref[...] = root_ref[...]
-        right_ref[0:half, :] = first
-        right_ref[half:order, :] = pack_ref[half:order, :]
+        right_ref[...] = pack_ref[half:order, :]
+        own_total(first)
 
     @pl.when(side != 0)
     def _():
-        right_ref[...] = root_ref[:, half:order]
+        right_ref[...] = root_ref[0:half, half:order]
         diagonal = pack_ref[order : order + 16, :].astype(jnp.float32)[0:1, :]
         second = jnp.where(rows > cols, tri, jnp.where(rows == cols, diagonal, tri_flipped))
         left_ref[0:half, 0:half] = first
         left_ref[half:order, half:order] = second.astype(jnp.bfloat16)
         left_ref[half:order, 0:half] = pack_ref[half:order, :]
         left_ref[0:half, half:order] = flip(pack_ref[half:order, :])
-
-    partial_ref[...] = dot(left_ref[...], own_ref[...]).astype(jnp.bfloat16)
+        own_total(root_ref[half:order, half:order])
 
 
 def own_part(half_group, root, pack, own):
@@ -149,37 +183,31 @@
         functools.partial(own_kernel, half_group),
         out_shape=(
             jax.ShapeDtypeStruct((order, order), jnp.bfloat16),
-            jax.ShapeDtypeStruct((order, half), jnp.bfloat16),
-            jax.ShapeDtypeStruct((order, half), jnp.bfloat16),
+            jax.ShapeDtypeStruct((half, half), jnp.bfloat16),
+            jax.ShapeDtypeStruct((order, half), jnp.float32),
         ),
         in_specs=[VMEM] * 3,
         out_specs=(VMEM,) * 3,
         compiler_params=pltpu.CompilerParams(vmem_limit_bytes=16 * MIB),
-        cost_estimate=pl.CostEstimate(flops=order**3, bytes_accessed=6 * order**2, transcendentals=0),
+        cost_estimate=pl.CostEstimate(flops=2 * order**3, bytes_accessed=7 * order**2, transcendentals=0),
     )(root, pack, own)
 
 
-def result_kernel(half_group, left_ref, right_ref, partial_ref, other_ref, out_ref):
-    order = left_ref.shape[0]
-    half = order // 2
-    side = lax.axis_index("dp") // half_group
-    mine = pl.ds(pl.multiple_of(side * half, half), half)
-    theirs = pl.ds(pl.multiple_of((1 - side) * half, half), half)
-    other_partial = dot(left_ref[...], other_ref[...]).astype(jnp.bfloat16)
-    total = dot(partial_ref[...], right_ref[mine, :]) + dot(other_partial, right_ref[theirs, :])
-    out_ref[...] = total.astype(jnp.bfloat16)
-
-
-def result_half(half_group, left, right, partial, other):
+def result_kernel(left_ref, right_ref, total_ref, other_ref, out_ref):
+    partial = dot(left_ref[...], other_ref[...]).astype(jnp.bfloat16)
+    out_ref[...] = (total_ref[...] + dot(partial, right_ref[...])).astype(jnp.bfloat16)
+
+
+def result_half(left, right, total, other):
     order = left.shape[0]
     return pl.pallas_call(
-        functools.partial(result_kernel, half_group),
+        result_kernel,
         out_shape=jax.ShapeDtypeStruct(other.shape, jnp.bfloat16),
         in_specs=[VMEM] * 4,
         out_specs=VMEM,
         compiler_params=pltpu.CompilerParams(vmem_limit_bytes=16 * MIB),
         cost_estimate=pl.CostEstimate(flops=2 * order**3, bytes_accessed=6 * order**2, transcendentals=0),
-    )(left, right, partial, other)
+    )(left, right, total, other)
 
 
 def stats_kernel(half_group, stat_ref, own_ref, other_ref, out_ref):
@@ -224,20 +252,21 @@
     dp_count = lax.axis_size("dp")
     half_group = dp_count // 2
     swap = [(source, (source + half_group) % dp_count) for source in range(dp_count)]
-    stat = statistics[0, 0, 0]
-    outgoing = move_blocks(to_slots_kernel, half_group, owner_table, gradient[0, 0])
+    outgoing, stat, old, table = load(
+        half_group, owner_table, gradient[0, 0], statistics[0, 0, 0], inv_roots[0, 0, 0]
+    )
     received = lax.all_to_all(outgoing, "fsdp", split_axis=0, concat_axis=0, tiled=True)
     own = received.reshape(order, half)
-    root, pack = fresh_and_packed(refresh, stat, inv_roots[0, 0, 0])
+    root, pack = fresh_and_packed(refresh, stat, old)
     other_pack = lax.ppermute(pack, "dp", swap)
     own, pack = lax.optimization_barrier((own, pack))
     other = lax.ppermute(own, "dp", swap)
-    left, right, partial = own_part(half_group, root, other_pack, own)
-    result = result_half(half_group, left, right, partial, other)
+    left, right, total = own_part(half_group, root, other_pack, own)
+    result = result_half(left, right, total, other)
     result, own, other = lax.optimization_barrier((result, own, other))
     returned = lax.all_to_all(result.reshape(outgoing.shape), "fsdp", split_axis=0, concat_axis=0, tiled=True)
     new_stat = updated_stats(half_group, stat, own, other)
-    update = move_blocks(from_slots_kernel, half_group, owner_table, returned)
+    update = from_slots(half_group, table, returned)
     return update[None, None], new_stat[None, None, None]
 
 

time: 92.6 us -> 89.2 us (0.963)
  local copies, waits for them, and re-layouts: 2.76 us -> 0 us
    unnamed x10 -> x0, local copies, waits for them, and re-layouts: 2.76 us -> none
    ppermute x1, waiting for transfers between devices: 6.71 us -> 5.35 us  [shards(): other = lax.ppermute(own, 'dp', swap)]
    all_to_all x1, waiting for transfers between devices: 8.83 us -> 9.87 us  [shards(): lax.all_to_all(outgoing, 'fsdp', split_axis=0, concat_axis=0, tiled=True)]
where the time goes in v2:
time: 89.2 us; the launch traced here: 88.3 us
  starting transfers between devices  48.9 us (55%)
  waiting for transfers between devices  32.1 us (36%)
  Pallas kernels  5.99 us (7%)
  between operations  1.34 us (2%)
    all_to_all x1, starting transfers between devices, shards(): lax.all_to_all(outgoing, 'fsdp', split_axis=0, concat_axis=0, tiled=True)  18.9 us
    all_to_all x1, waiting for transfers between devices, shards(): lax.all_to_all(result.reshape(outgoing.shape), 'fsdp', split_axis=0, conc...  16.9 us
    all_to_all x1, starting transfers between devices, shards(): lax.all_to_all(result.reshape(outgoing.shape), 'fsdp', split_axis=0, conc...  14.5 us
    all_to_all x1, waiting for transfers between devices, shards(): lax.all_to_all(outgoing, 'fsdp', split_axis=0, concat_axis=0, tiled=True)  9.87 us
    ppermute x1, starting transfers between devices, shards(): other_pack = lax.ppermute(pack, 'dp', swap)  7.73 us
    ppermute x1, starting transfers between devices, shards(): other = lax.ppermute(own, 'dp', swap)  7.72 us
    ppermute x1, waiting for transfers between devices, shards(): other = lax.ppermute(own, 'dp', swap)  5.35 us
    pallas_call x1, Pallas kernels, load(): pl.pallas_call(functools.partial(load_kernel, groups), out_shape=(pltpu.H...  1.81 us
  transfers between devices with their start and end apart: 4, of which 3 were waited for; matrix products, arithmetic and copies ran while one was open for 0% of the time, Pallas kernels for 2%

profile of v2, /device:TPU:6, one launch (start us, length us, event | category | flops | bytes accessed | tf_op | source)
XLA Modules:
  0.0 88.3 jit_solution(16136207235307409585)
XLA Ops:
  0.6 1.8 %shard_map.68 = (bf16[16,32,256]{2,1,0:T(8,128)(2,1)}, f32[512,512]{1,0:T(8,128)S(1)}, bf16[512,512]{1,0:T(8,128)(2,1)S(1)}, s32[8,1,16]{2,1,0:T(1,128)S(4)}) custom-call(s32[8,1,16]{2,1,0:T(1,128)} %table_ref.1, bf16[16,32,256]{2,1,0:T(8,128)(2,1)} %bitcast.13, f32[512,512]{1,0:T(8,128)} %bitcast.10, bf16[512,512]{1,0:T(8,128)(2,1)} %bitcast.12), custom_call_target="tpu_custom_call" | custom-call | bytes 2097152 | tf_op jit(solution)/shard_map/pallas_call | solution.py:49
  2.5 18.9 %all-to-all-start = ((bf16[16,32,256]{2,1,0:T(8,128)(2,1)}), bf16[16,32,256]{2,1,0:T(8,128)(2,1)S(1)}, u32[]{:S(2)}, u32[]{:S(2)}) async-start(bf16[16,32,256]{2,1,0:T(8,128)(2,1)} %get-tuple-element.20), calls=%async_computation | async-start | bytes 524288 | tf_op jit(solution)/shard_map/all_to_all | solution.py:258
  22.0 0.1 shard_map.69
  22.1 7.7 %collective-permute-start = (bf16[528,256]{1,0:T(8,128)(2,1)S(1)}, bf16[528,256]{1,0:T(8,128)(2,1)S(1)}, u32[]{:S(2)}, u32[]{:S(2)}) collective-permute-start(bf16[528,256]{1,0:T(8,128)(2,1)S(1)} %get-tuple-element.19), channel_id=1, source_target_pairs={{0,512},{64,576},{128,640},{192,704},{256,768},{320,832},{384,896}... | collective-permute-start | bytes 811016 | tf_op jit(solution)/shard_map/ppermute | solution.py:261
  29.8 9.9 %all-to-all-done = bf16[16,32,256]{2,1,0:T(8,128)(2,1)S(1)} async-done(((bf16[16,32,256]{2,1,0:T(8,128)(2,1)}), bf16[16,32,256]{2,1,0:T(8,128)(2,1)S(1)}, u32[]{:S(2)}, u32[]{:S(2)}) %all-to-all-start) | async-done | bytes 262176 | tf_op jit(solution)/shard_map/all_to_all | solution.py:258
  39.7 7.7 %collective-permute-start.1 = (bf16[512,256]{1,0:T(8,128)(2,1)S(1)}, bf16[512,256]{1,0:T(8,128)(2,1)S(1)}, u32[]{:S(2)}, u32[]{:S(2)}) collective-permute-start(bf16[512,256]{1,0:T(8,128)(2,1)S(1)} %bitcast.7), channel_id=1, source_target_pairs={{0,512},{64,576},{128,640},{192,704},{256,768},{320,832},{384,896}... | collective-permute-start | bytes 786440 | tf_op jit(solution)/shard_map/ppermute | solution.py:263
  47.4 0.0 collective-permute-done.pack_ref
  47.4 0.6 shard_map.70
  48.0 5.4 %collective-permute-done.1.other_ref = bf16[512,256]{1,0:T(8,128)(2,1)S(1)} collective-permute-done((bf16[512,256]{1,0:T(8,128)(2,1)S(1)}, bf16[512,256]{1,0:T(8,128)(2,1)S(1)}, u32[]{:S(2)}, u32[]{:S(2)}) %collective-permute-start.1) | collective-permute-done | bytes 262176 | tf_op jit(solution)/shard_map/ppermute | solution.py:263
  53.4 1.2 %shard_map.71 = bf16[512,256]{1,0:T(8,128)(2,1)} custom-call(bf16[512,512]{1,0:T(8,128)(2,1)S(1)} %get-tuple-element.22.left_ref, bf16[256,256]{1,0:T(8,128)(2,1)S(1)} %get-tuple-element.23.right_ref, f32[512,256]{1,0:T(8,128)S(1)} %get-tuple-element.24.total_ref, bf16[512,256]{1,0:T(8,128)(2,1)S(1)} %collective-permute-done.1.other_ref), custom_call_target="tpu_custom_call" | custom-call | flops 268435456 | bytes 1572864 | tf_op jit(solution)/shard_map/pallas_call | solution.py:203
  54.6 14.5 %all-to-all-start.1 = ((bf16[16,32,256]{2,1,0:T(8,128)(2,1)}), bf16[16,32,256]{2,1,0:T(8,128)(2,1)S(1)}, u32[]{:S(2)}, u32[]{:S(2)}) async-start(bf16[16,32,256]{2,1,0:T(8,128)(2,1)} %bitcast.4), calls=%async_computation.1 | async-start | bytes 524288 | tf_op jit(solution)/shard_map/all_to_all | solution.py:267
  69.1 1.5 %shard_map.73 = f32[512,512]{1,0:T(8,128)} custom-call(f32[512,512]{1,0:T(8,128)S(1)} %get-tuple-element.16.stat_ref, bf16[512,256]{1,0:T(8,128)(2,1)S(1)} %bitcast.9, bf16[512,256]{1,0:T(8,128)(2,1)S(1)} %collective-permute-done.1.other_ref), custom_call_target="tpu_custom_call" | custom-call | flops 268435456 | bytes 2621440 | tf_op jit(solution)/shard_map/pallas_call | solution.py:239
  70.6 16.9 %all-to-all-done.1.got_ref = bf16[16,32,256]{2,1,0:T(8,128)(2,1)S(1)} async-done(((bf16[16,32,256]{2,1,0:T(8,128)(2,1)}), bf16[16,32,256]{2,1,0:T(8,128)(2,1)S(1)}, u32[]{:S(2)}, u32[]{:S(2)}) %all-to-all-start.1) | async-done | bytes 262176 | tf_op jit(solution)/shard_map/all_to_all | solution.py:267
  87.5 0.8 shard_map.72
Async XLA Ops:
  2.5 37.2 %all-to-all-start = ((bf16[16,32,256]{2,1,0:T(8,128)(2,1)}), bf16[16,32,256]{2,1,0:T(8,128)(2,1)S(1)}, u32[]{:S(2)}, u32[]{:S(2)}) async-start(bf16[16,32,256]{2,1,0:T(8,128)(2,1)} %get-tuple-element.20), calls=%async_computation | async-start | bytes 524288 | tf_op jit(solution)/shard_map/all_to_all | solution.py:258
  22.1 25.3 %collective-permute-start = (bf16[528,256]{1,0:T(8,128)(2,1)S(1)}, bf16[528,256]{1,0:T(8,128)(2,1)S(1)}, u32[]{:S(2)}, u32[]{:S(2)}) collective-permute-start(bf16[528,256]{1,0:T(8,128)(2,1)S(1)} %get-tuple-element.19), channel_id=1, source_target_pairs={{0,512},{64,576},{128,640},{192,704},{256,768},{320,832},{384,896}... | collective-permute-start | bytes 811016 | tf_op jit(solution)/shard_map/ppermute | solution.py:261
  39.7 13.7 %collective-permute-start.1 = (bf16[512,256]{1,0:T(8,128)(2,1)S(1)}, bf16[512,256]{1,0:T(8,128)(2,1)S(1)}, u32[]{:S(2)}, u32[]{:S(2)}) collective-permute-start(bf16[512,256]{1,0:T(8,128)(2,1)S(1)} %bitcast.7), channel_id=1, source_target_pairs={{0,512},{64,576},{128,640},{192,704},{256,768},{320,832},{384,896}... | collective-permute-start | bytes 786440 | tf_op jit(solution)/shard_map/ppermute | solution.py:263
  54.6 32.9 %all-to-all-start.1 = ((bf16[16,32,256]{2,1,0:T(8,128)(2,1)}), bf16[16,32,256]{2,1,0:T(8,128)(2,1)S(1)}, u32[]{:S(2)}, u32[]{:S(2)}) async-start(bf16[16,32,256]{2,1,0:T(8,128)(2,1)} %bitcast.4), calls=%async_computation.1 | async-start | bytes 524288 | tf_op jit(solution)/shard_map/all_to_all | solution.py:267

commit v3 on v2

--- a/solution.py
+++ b/solution.py
@@ -10,6 +10,7 @@
 ITERS = 2
 STAT_DECAY = 0.9
 MIB = 1024 * 1024
+ORDER_16 = (12, 11, 7, 13, 6, 0, 8, 3, 9, 4, 10, 2, 5, 14, 15, 1)
 
 VMEM = pl.BlockSpec(memory_space=pltpu.VMEM)
 SMEM = pl.BlockSpec(memory_space=pltpu.SMEM)
@@ -20,11 +21,15 @@
     return lax.dot_general(left, right, (contract, ((), ())), preferred_element_type=jnp.float32)
 
 
+def device_order(count):
+    return ORDER_16 if count == len(ORDER_16) else tuple(range(count))
+
+
 def flip(block):
     return block.astype(jnp.float32).T.astype(block.dtype)
 
 
-def load_kernel(groups, table_ref, grad_ref, stat_ref, old_ref, out_ref, stat_out, old_out, table_out, held, sems, move_sems):
+def load_kernel(groups, table_ref, grad_ref, stat_ref, old_ref, out_ref, stat_out, old_out, table_out, held, place, sems, move_sems):
     copies = [
         pltpu.make_async_copy(source, target, sems.at[i])
         for i, (source, target) in enumerate(
@@ -33,12 +38,14 @@
     ]
     for copy in copies:
         copy.start()
+    for position, device in enumerate(device_order(held.shape[0])):
+        place[device] = position
     group = lax.rem(lax.axis_index("dp"), groups)
     copies[0].wait()
     copies[1].wait()
     moves = []
     for r in range(held.shape[0]):
-        moves.append(pltpu.make_async_copy(held.at[r], out_ref.at[table_out[group, 0, r]], move_sems.at[r]))
+        moves.append(pltpu.make_async_copy(held.at[r], out_ref.at[place[table_out[group, 0, r]]], move_sems.at[r]))
         moves[-1].start()
     for copy in copies[2:] + moves:
         copy.wait()
@@ -58,6 +65,7 @@
         out_specs=(HBM, VMEM, VMEM, SMEM),
         scratch_shapes=[
             pltpu.VMEM(grad.shape, grad.dtype),
+            pltpu.SMEM((grad.shape[0],), jnp.int32),
             pltpu.SemaphoreType.DMA((4,)),
             pltpu.SemaphoreType.DMA((grad.shape[0],)),
         ],
@@ -144,7 +152,7 @@
     )(flag, stat, old)
 
 
-def own_kernel(half_group, root_ref, pack_ref, own_ref, left_ref, right_ref, total_ref):
+def own_kernel(half_group, slots, root_ref, pack_ref, own_ref, left_ref, right_ref, total_ref, whole):
     order = root_ref.shape[0]
     half = order // 2
     side = lax.axis_index("dp") // half_group
@@ -154,13 +162,22 @@
     tri_flipped = tri.T
     first = jnp.where(rows <= cols, tri, tri_flipped).astype(jnp.bfloat16)
 
+    slab = order // slots
+    arrived = lax.broadcasted_iota(jnp.int32, (1, order), 1)
+    source = jnp.zeros_like(arrived)
+    for position, device in enumerate(device_order(slots)):
+        inside = (arrived >= position * slab) & (arrived < (position + 1) * slab)
+        source = jnp.where(inside, arrived + (device - position) * slab, source)
+    lines = lax.broadcasted_iota(jnp.int32, (order, order), 0)
+    to_arrived = jnp.where(lines == source, 1.0, 0.0).astype(jnp.bfloat16)
+
     def own_total(right_own):
         partial = dot(left_ref[...], own_ref[...]).astype(jnp.bfloat16)
         total_ref[...] = dot(partial, right_own)
 
     @pl.when(side == 0)
     def _():
-        left_ref[...] = root_ref[...]
+        left_ref[...] = dot(root_ref[...], to_arrived).astype(jnp.bfloat16)
         right_ref[...] = pack_ref[half:order, :]
         own_total(first)
 
@@ -169,18 +186,19 @@
         right_ref[...] = root_ref[0:half, half:order]
         diagonal = pack_ref[order : order + 16, :].astype(jnp.float32)[0:1, :]
         second = jnp.where(rows > cols, tri, jnp.where(rows == cols, diagonal, tri_flipped))
-        left_ref[0:half, 0:half] = first
-        left_ref[half:order, half:order] = second.astype(jnp.bfloat16)
-        left_ref[half:order, 0:half] = pack_ref[half:order, :]
-        left_ref[0:half, half:order] = flip(pack_ref[half:order, :])
+        whole[0:half, 0:half] = first
+        whole[half:order, half:order] = second.astype(jnp.bfloat16)
+        whole[half:order, 0:half] = pack_ref[half:order, :]
+        whole[0:half, half:order] = flip(pack_ref[half:order, :])
+        left_ref[...] = dot(whole[...], to_arrived).astype(jnp.bfloat16)
         own_total(root_ref[half:order, half:order])
 
 
-def own_part(half_group, root, pack, own):
+def own_part(half_group, slots, root, pack, own):
     order = root.shape[0]
     half = order // 2
     return pl.pallas_call(
-        functools.partial(own_kernel, half_group),
+        functools.partial(own_kernel, half_group, slots),
         out_shape=(
             jax.ShapeDtypeStruct((order, order), jnp.bfloat16),
             jax.ShapeDtypeStruct((half, half), jnp.bfloat16),
@@ -188,8 +206,9 @@
         ),
         in_specs=[VMEM] * 3,
         out_specs=(VMEM,) * 3,
+        scratch_shapes=[pltpu.VMEM((order, order), jnp.bfloat16)],
         compiler_params=pltpu.CompilerParams(vmem_limit_bytes=16 * MIB),
-        cost_estimate=pl.CostEstimate(flops=2 * order**3, bytes_accessed=7 * order**2, transcendentals=0),
+        cost_estimate=pl.CostEstimate(flops=4 * order**3, bytes_accessed=7 * order**2, transcendentals=0),
     )(root, pack, own)
 
 
@@ -210,7 +229,7 @@
     )(left, right, total, other)
 
 
-def stats_kernel(half_group, stat_ref, own_ref, other_ref, out_ref):
+def stats_kernel(half_group, slots, stat_ref, own_ref, other_ref, out_ref, sorted_own, sorted_other):
     order = stat_ref.shape[0]
     half = order // 2
     side = lax.axis_index("dp") // half_group
@@ -218,7 +237,13 @@
 
     @pl.when(side == 0)
     def _():
-        own, other = own_ref[...], other_ref[...]
+        slab = order // slots
+        for position, device in enumerate(device_order(slots)):
+            arrived = slice(position * slab, (position + 1) * slab)
+            lines = slice(device * slab, (device + 1) * slab)
+            sorted_own[lines, :] = own_ref[arrived, :]
+            sorted_other[lines, :] = other_ref[arrived, :]
+        own, other = sorted_own[...], sorted_other[...]
         gram = dot(own, own, ((1,), (1,))) + dot(other, other, ((1,), (1,)))
         out_ref[...] = STAT_DECAY * stat_ref[...] + factor * gram
 
@@ -234,13 +259,14 @@
                 out_ref[lines, columns] = STAT_DECAY * stat_ref[lines, columns] + factor * gram
 
 
-def updated_stats(half_group, stat, own, other):
+def updated_stats(half_group, slots, stat, own, other):
     order = stat.shape[0]
     return pl.pallas_call(
-        functools.partial(stats_kernel, half_group),
+        functools.partial(stats_kernel, half_group, slots),
         out_shape=jax.ShapeDtypeStruct(stat.shape, jnp.float32),
         in_specs=[VMEM] * 3,
         out_specs=VMEM,
+        scratch_shapes=[pltpu.VMEM(own.shape, own.dtype)] * 2,
         compiler_params=pltpu.CompilerParams(vmem_limit_bytes=16 * MIB),
         cost_estimate=pl.CostEstimate(flops=2 * order**3, bytes_accessed=10 * order**2, transcendentals=0),
     )(stat, own, other)
@@ -250,22 +276,25 @@
     order = statistics.shape[-1]
     half = order // 2
     dp_count = lax.axis_size("dp")
+    slots = lax.axis_size("fsdp")
     half_group = dp_count // 2
     swap = [(source, (source + half_group) % dp_count) for source in range(dp_count)]
     outgoing, stat, old, table = load(
         half_group, owner_table, gradient[0, 0], statistics[0, 0, 0], inv_roots[0, 0, 0]
     )
-    received = lax.all_to_all(outgoing, "fsdp", split_axis=0, concat_axis=0, tiled=True)
+    received = lax.all_to_all(
+        outgoing, "fsdp", split_axis=0, concat_axis=0, tiled=True, axis_index_groups=[list(device_order(slots))]
+    )
     own = received.reshape(order, half)
     root, pack = fresh_and_packed(refresh, stat, old)
     other_pack = lax.ppermute(pack, "dp", swap)
     own, pack = lax.optimization_barrier((own, pack))
     other = lax.ppermute(own, "dp", swap)
-    left, right, total = own_part(half_group, root, other_pack, own)
+    left, right, total = own_part(half_group, slots, root, other_pack, own)
     result = result_half(left, right, total, other)
     result, own, other = lax.optimization_barrier((result, own, other))
     returned = lax.all_to_all(result.reshape(outgoing.shape), "fsdp", split_axis=0, concat_axis=0, tiled=True)
-    new_stat = updated_stats(half_group, stat, own, other)
+    new_stat = updated_stats(half_group, slots, stat, own, other)
     update = from_slots(half_group, table, returned)
     return update[None, None], new_stat[None, None, None]
 

time: 89.2 us -> 87.1 us (0.976)
  the two profiles are of different devices: /device:TPU:6 before, /device:TPU:4 now
where the time goes in v3:
time: 87.1 us; the launch traced here: 86.3 us
  starting transfers between devices  45.6 us (52%)
  waiting for transfers between devices  33 us (38%)
  Pallas kernels  6.34 us (7%)
  between operations  1.34 us (2%)
    all_to_all x1, starting transfers between devices, shards(): lax.all_to_all(outgoing, 'fsdp', split_axis=0, concat_axis=0, tiled=True,...  20.9 us
    all_to_all x1, waiting for transfers between devices, shards(): lax.all_to_all(result.reshape(outgoing.shape), 'fsdp', split_axis=0, conc...  16.3 us
    ppermute x1, waiting for transfers between devices, shards(): other = lax.ppermute(own, 'dp', swap)  10.3 us
    all_to_all x1, starting transfers between devices, shards(): lax.all_to_all(result.reshape(outgoing.shape), 'fsdp', split_axis=0, conc...  9.24 us
    ppermute x1, starting transfers between devices, shards(): other_pack = lax.ppermute(pack, 'dp', swap)  7.73 us
    ppermute x1, starting transfers between devices, shards(): other = lax.ppermute(own, 'dp', swap)  7.72 us
    all_to_all x1, waiting for transfers between devices, shards(): lax.all_to_all(outgoing, 'fsdp', split_axis=0, concat_axis=0, tiled=True,...  6.44 us
    pallas_call x1, Pallas kernels, load(): pl.pallas_call(functools.partial(load_kernel, groups), out_shape=(pltpu.H...  1.81 us
  transfers between devices with their start and end apart: 4, of which 3 were waited for; matrix products, arithmetic and copies ran while one was open for 0% of the time, Pallas kernels for 3%

profile of v3, /device:TPU:4, one launch (start us, length us, event | category | flops | bytes accessed | tf_op | source)
XLA Modules:
  0.0 86.3 jit_solution(2927556921214255335)
XLA Ops:
  0.6 1.8 %shard_map.68 = (bf16[16,32,256]{2,1,0:T(8,128)(2,1)}, f32[512,512]{1,0:T(8,128)S(1)}, bf16[512,512]{1,0:T(8,128)(2,1)S(1)}, s32[8,1,16]{2,1,0:T(1,128)S(4)}) custom-call(s32[8,1,16]{2,1,0:T(1,128)} %table_ref.1, bf16[16,32,256]{2,1,0:T(8,128)(2,1)} %bitcast.13, f32[512,512]{1,0:T(8,128)} %bitcast.10, bf16[512,512]{1,0:T(8,128)(2,1)} %bitcast.12), custom_call_target="tpu_custom_call" | custom-call | bytes 2097152 | tf_op jit(solution)/shard_map/pallas_call | solution.py:56
  2.5 20.9 %all-to-all-start = ((bf16[16,32,256]{2,1,0:T(8,128)(2,1)}), bf16[16,32,256]{2,1,0:T(8,128)(2,1)S(1)}, u32[]{:S(2)}, u32[]{:S(2)}) async-start(bf16[16,32,256]{2,1,0:T(8,128)(2,1)} %get-tuple-element.20), calls=%async_computation | async-start | bytes 524288 | tf_op jit(solution)/shard_map/all_to_all | solution.py:285
  24.0 0.1 shard_map.69
  24.1 7.7 %collective-permute-start = (bf16[528,256]{1,0:T(8,128)(2,1)S(1)}, bf16[528,256]{1,0:T(8,128)(2,1)S(1)}, u32[]{:S(2)}, u32[]{:S(2)}) collective-permute-start(bf16[528,256]{1,0:T(8,128)(2,1)S(1)} %get-tuple-element.19), channel_id=1, source_target_pairs={{0,512},{64,576},{128,640},{192,704},{256,768},{320,832},{384,896}... | collective-permute-start | bytes 811016 | tf_op jit(solution)/shard_map/ppermute | solution.py:290
  31.8 6.4 %all-to-all-done = bf16[16,32,256]{2,1,0:T(8,128)(2,1)S(1)} async-done(((bf16[16,32,256]{2,1,0:T(8,128)(2,1)}), bf16[16,32,256]{2,1,0:T(8,128)(2,1)S(1)}, u32[]{:S(2)}, u32[]{:S(2)}) %all-to-all-start) | async-done | bytes 262176 | tf_op jit(solution)/shard_map/all_to_all | solution.py:285
  38.3 7.7 %collective-permute-start.1 = (bf16[512,256]{1,0:T(8,128)(2,1)S(1)}, bf16[512,256]{1,0:T(8,128)(2,1)S(1)}, u32[]{:S(2)}, u32[]{:S(2)}) collective-permute-start(bf16[512,256]{1,0:T(8,128)(2,1)S(1)} %bitcast.7), channel_id=1, source_target_pairs={{0,512},{64,576},{128,640},{192,704},{256,768},{320,832},{384,896}... | collective-permute-start | bytes 786440 | tf_op jit(solution)/shard_map/ppermute | solution.py:292
  46.0 0.0 collective-permute-done.pack_ref
  46.0 0.9 %shard_map.70 = (bf16[512,512]{1,0:T(8,128)(2,1)S(1)}, bf16[256,256]{1,0:T(8,128)(2,1)S(1)}, f32[512,256]{1,0:T(8,128)S(1)}) custom-call(bf16[512,512]{1,0:T(8,128)(2,1)S(1)} %get-tuple-element.18.root_ref, bf16[528,256]{1,0:T(8,128)(2,1)S(1)} %collective-permute-done.pack_ref, bf16[512,256]{1,0:T(8,128)(2,1)S(1)} %bitcast.8), custom_call_target="tpu_custom_call" | custom-call | flops 536870912 | bytes 1835008 | tf_op jit(solution)/shard_map/pallas_call | solution.py:200
  47.0 10.3 %collective-permute-done.1.other_ref = bf16[512,256]{1,0:T(8,128)(2,1)S(1)} collective-permute-done((bf16[512,256]{1,0:T(8,128)(2,1)S(1)}, bf16[512,256]{1,0:T(8,128)(2,1)S(1)}, u32[]{:S(2)}, u32[]{:S(2)}) %collective-permute-start.1) | collective-permute-done | bytes 262176 | tf_op jit(solution)/shard_map/ppermute | solution.py:292
  57.2 1.2 %shard_map.71 = bf16[512,256]{1,0:T(8,128)(2,1)} custom-call(bf16[512,512]{1,0:T(8,128)(2,1)S(1)} %get-tuple-element.22.left_ref, bf16[256,256]{1,0:T(8,128)(2,1)S(1)} %get-tuple-element.23.right_ref, f32[512,256]{1,0:T(8,128)S(1)} %get-tuple-element.24.total_ref, bf16[512,256]{1,0:T(8,128)(2,1)S(1)} %collective-permute-done.1.other_ref), custom_call_target="tpu_custom_call" | custom-call | flops 268435456 | bytes 1572864 | tf_op jit(solution)/shard_map/pallas_call | solution.py:222
  58.4 9.2 %all-to-all-start.1 = ((bf16[16,32,256]{2,1,0:T(8,128)(2,1)}), bf16[16,32,256]{2,1,0:T(8,128)(2,1)S(1)}, u32[]{:S(2)}, u32[]{:S(2)}) async-start(bf16[16,32,256]{2,1,0:T(8,128)(2,1)} %bitcast.4), calls=%async_computation.1 | async-start | bytes 524288 | tf_op jit(solution)/shard_map/all_to_all | solution.py:296
  67.7 1.5 %shard_map.73 = f32[512,512]{1,0:T(8,128)} custom-call(f32[512,512]{1,0:T(8,128)S(1)} %get-tuple-element.16.stat_ref, bf16[512,256]{1,0:T(8,128)(2,1)S(1)} %bitcast.9, bf16[512,256]{1,0:T(8,128)(2,1)S(1)} %collective-permute-done.1.other_ref), custom_call_target="tpu_custom_call" | custom-call | flops 268435456 | bytes 2621440 | tf_op jit(solution)/shard_map/pallas_call | solution.py:264
  69.2 16.3 %all-to-all-done.1.got_ref = bf16[16,32,256]{2,1,0:T(8,128)(2,1)S(1)} async-done(((bf16[16,32,256]{2,1,0:T(8,128)(2,1)}), bf16[16,32,256]{2,1,0:T(8,128)(2,1)S(1)}, u32[]{:S(2)}, u32[]{:S(2)}) %all-to-all-start.1) | async-done | bytes 262176 | tf_op jit(solution)/shard_map/all_to_all | solution.py:296
  85.5 0.8 shard_map.72
Async XLA Ops:
  2.5 35.8 %all-to-all-start = ((bf16[16,32,256]{2,1,0:T(8,128)(2,1)}), bf16[16,32,256]{2,1,0:T(8,128)(2,1)S(1)}, u32[]{:S(2)}, u32[]{:S(2)}) async-start(bf16[16,32,256]{2,1,0:T(8,128)(2,1)} %get-tuple-element.20), calls=%async_computation | async-start | bytes 524288 | tf_op jit(solution)/shard_map/all_to_all | solution.py:285
  24.1 21.9 %collective-permute-start = (bf16[528,256]{1,0:T(8,128)(2,1)S(1)}, bf16[528,256]{1,0:T(8,128)(2,1)S(1)}, u32[]{:S(2)}, u32[]{:S(2)}) collective-permute-start(bf16[528,256]{1,0:T(8,128)(2,1)S(1)} %get-tuple-element.19), channel_id=1, source_target_pairs={{0,512},{64,576},{128,640},{192,704},{256,768},{320,832},{384,896}... | collective-permute-start | bytes 811016 | tf_op jit(solution)/shard_map/ppermute | solution.py:290
  38.3 19.0 %collective-permute-start.1 = (bf16[512,256]{1,0:T(8,128)(2,1)S(1)}, bf16[512,256]{1,0:T(8,128)(2,1)S(1)}, u32[]{:S(2)}, u32[]{:S(2)}) collective-permute-start(bf16[512,256]{1,0:T(8,128)(2,1)S(1)} %bitcast.7), channel_id=1, source_target_pairs={{0,512},{64,576},{128,640},{192,704},{256,768},{320,832},{384,896}... | collective-permute-start | bytes 786440 | tf_op jit(solution)/shard_map/ppermute | solution.py:292
  58.4 27.0 %all-to-all-start.1 = ((bf16[16,32,256]{2,1,0:T(8,128)(2,1)}), bf16[16,32,256]{2,1,0:T(8,128)(2,1)S(1)}, u32[]{:S(2)}, u32[]{:S(2)}) async-start(bf16[16,32,256]{2,1,0:T(8,128)(2,1)} %bitcast.4), calls=%async_computation.1 | async-start | bytes 524288 | tf_op jit(solution)/shard_map/all_to_all | solution.py:296

commit v4 on v3

--- a/solution.py
+++ b/solution.py
@@ -29,11 +29,11 @@
     return block.astype(jnp.float32).T.astype(block.dtype)
 
 
-def load_kernel(groups, table_ref, grad_ref, stat_ref, old_ref, out_ref, stat_out, old_out, table_out, held, place, sems, move_sems):
+def load_kernel(groups, table_ref, grad_ref, out_ref, table_out, held, place, sems, move_sems):
     copies = [
         pltpu.make_async_copy(source, target, sems.at[i])
         for i, (source, target) in enumerate(
-            ((table_ref, table_out), (grad_ref, held), (stat_ref, stat_out), (old_ref, old_out))
+            ((table_ref, table_out), (grad_ref, held))
         )
     ]
     for copy in copies:
@@ -47,31 +47,29 @@
     for r in range(held.shape[0]):
         moves.append(pltpu.make_async_copy(held.at[r], out_ref.at[place[table_out[group, 0, r]]], move_sems.at[r]))
         moves[-1].start()
-    for copy in copies[2:] + moves:
+    for copy in moves:
         copy.wait()
 
 
-def load(groups, table, grad, stat, old):
-    size = 2 * grad.size * 2 + 4 * stat.size + 2 * old.size
+def load(groups, table, grad):
+    size = 2 * grad.size * 2
     return pl.pallas_call(
         functools.partial(load_kernel, groups),
         out_shape=(
             pltpu.HBM(grad.shape, grad.dtype),
-            pltpu.VMEM(stat.shape, stat.dtype),
-            pltpu.VMEM(old.shape, old.dtype),
             pltpu.SMEM(table.shape, table.dtype),
         ),
-        in_specs=[HBM] * 4,
-        out_specs=(HBM, VMEM, VMEM, SMEM),
+        in_specs=[HBM] * 2,
+        out_specs=(HBM, SMEM),
         scratch_shapes=[
             pltpu.VMEM(grad.shape, grad.dtype),
             pltpu.SMEM((grad.shape[0],), jnp.int32),
-            pltpu.SemaphoreType.DMA((4,)),
+            pltpu.SemaphoreType.DMA((2,)),
             pltpu.SemaphoreType.DMA((grad.shape[0],)),
         ],
         compiler_params=pltpu.CompilerParams(vmem_limit_bytes=4 * MIB),
         cost_estimate=pl.CostEstimate(flops=0, bytes_accessed=size, transcendentals=0),
-    )(*(pltpu.with_memory_space_constraint(x, pltpu.HBM) for x in (table, grad, stat, old)))
+    )(*(pltpu.with_memory_space_constraint(x, pltpu.HBM) for x in (table, grad)))
 
 
 def from_slots_kernel(groups, table_ref, got_ref, out_ref, sems):
@@ -279,9 +277,8 @@
     slots = lax.axis_size("fsdp")
     half_group = dp_count // 2
     swap = [(source, (source + half_group) % dp_count) for source in range(dp_count)]
-    outgoing, stat, old, table = load(
-        half_group, owner_table, gradient[0, 0], statistics[0, 0, 0], inv_roots[0, 0, 0]
-    )
+    outgoing, table = load(half_group, owner_table, gradient[0, 0])
+    stat, old = statistics[0, 0, 0], inv_roots[0, 0, 0]
     received = lax.all_to_all(
         outgoing, "fsdp", split_axis=0, concat_axis=0, tiled=True, axis_index_groups=[list(device_order(slots))]
     )

time: 87.1 us -> 88.3 us (1.014)
  the two profiles are of different devices: /device:TPU:4 before, /device:TPU:6 now
where the time goes in v4:
time: 88.3 us; the launch traced here: 87.2 us
  starting transfers between devices  46.2 us (52%)
  waiting for transfers between devices  30.5 us (35%)
  Pallas kernels  7.98 us (9%)
  between operations  1.37 us (2%)
  local copies, waits for them, and re-layouts  1.23 us (1%)
    all_to_all x1, starting transfers between devices, shards(): lax.all_to_all(outgoing, 'fsdp', split_axis=0, concat_axis=0, tiled=True,...  20.9 us
    all_to_all x1, waiting for transfers between devices, shards(): lax.all_to_all(result.reshape(outgoing.shape), 'fsdp', split_axis=0, conc...  16.9 us
    all_to_all x1, starting transfers between devices, shards(): lax.all_to_all(result.reshape(outgoing.shape), 'fsdp', split_axis=0, conc...  11.5 us
    ppermute x1, waiting for transfers between devices, shards(): other = lax.ppermute(own, 'dp', swap)  8.42 us
    ppermute x1, starting transfers between devices, shards(): other = lax.ppermute(own, 'dp', swap)  7.72 us
    ppermute x1, starting transfers between devices, shards(): other_pack = lax.ppermute(pack, 'dp', swap)  6.11 us
    all_to_all x1, waiting for transfers between devices, shards(): lax.all_to_all(outgoing, 'fsdp', split_axis=0, concat_axis=0, tiled=True,...  5.22 us
    pallas_call x1, Pallas kernels, load(): pl.pallas_call(functools.partial(load_kernel, groups), out_shape=(pltpu.H...  1.85 us
  transfers between devices with their start and end apart: 4, of which 3 were waited for; matrix products, arithmetic and copies ran while one was open for 0% of the time, Pallas kernels for 5%

profile of v4, /device:TPU:6, one launch (start us, length us, event | category | flops | bytes accessed | tf_op | source)
XLA Modules:
  0.0 87.2 jit_solution(479797038445303847)
XLA Ops:
  0.6 0.0 copy-start.2
  0.6 1.9 %shard_map.68 = (bf16[16,32,256]{2,1,0:T(8,128)(2,1)}, s32[8,1,16]{2,1,0:T(1,128)S(4)}) custom-call(s32[8,1,16]{2,1,0:T(1,128)} %table_ref.1, bf16[16,32,256]{2,1,0:T(8,128)(2,1)} %bitcast.14), custom_call_target="tpu_custom_call" | custom-call | bytes 524288 | tf_op jit(solution)/shard_map/pallas_call | solution.py:56
  2.5 20.9 %all-to-all-start = ((bf16[16,32,256]{2,1,0:T(8,128)(2,1)}), bf16[16,32,256]{2,1,0:T(8,128)(2,1)S(1)}, u32[]{:S(2)}, u32[]{:S(2)}) async-start(bf16[16,32,256]{2,1,0:T(8,128)(2,1)} %get-tuple-element.16), calls=%async_computation | async-start | bytes 524288 | tf_op jit(solution)/shard_map/all_to_all | solution.py:282
  24.0 0.0 copy-done.2
  24.0 0.0 copy-start
  24.1 1.2 %copy-done = f32[1,1,1,512,512]{4,3,2,1,0:T(8,128)S(1)} copy-done((f32[1,1,1,512,512]{4,3,2,1,0:T(8,128)S(1)}, f32[1,1,1,512,512]{4,3,2,1,0:T(8,128)}, u32[]{:S(2)}) %copy-start) | copy-done | bytes 1048600
  25.3 1.7 %shard_map.69 = (bf16[512,512]{1,0:T(8,128)(2,1)S(1)}, bf16[528,256]{1,0:T(8,128)(2,1)S(1)}) custom-call(s32[1,1,1]{2,1,0:T(1,128)S(6)} %copy.7.flag_ref, f32[512,512]{1,0:T(8,128)S(1)} %bitcast.10, bf16[512,512]{1,0:T(8,128)(2,1)S(1)} %bitcast.12), custom_call_target="tpu_custom_call" | custom-call | flops 1073741824 | bytes 2359296 | tf_op jit(solution)/shard_map/pallas_call | solution.py:140
  27.0 6.1 %collective-permute-start = (bf16[528,256]{1,0:T(8,128)(2,1)S(1)}, bf16[528,256]{1,0:T(8,128)(2,1)S(1)}, u32[]{:S(2)}, u32[]{:S(2)}) collective-permute-start(bf16[528,256]{1,0:T(8,128)(2,1)S(1)} %get-tuple-element.15), channel_id=1, source_target_pairs={{0,512},{64,576},{128,640},{192,704},{256,768},{320,832},{384,896}... | collective-permute-start | bytes 811016 | tf_op jit(solution)/shard_map/ppermute | solution.py:287
  33.1 5.2 %all-to-all-done = bf16[16,32,256]{2,1,0:T(8,128)(2,1)S(1)} async-done(((bf16[16,32,256]{2,1,0:T(8,128)(2,1)}), bf16[16,32,256]{2,1,0:T(8,128)(2,1)S(1)}, u32[]{:S(2)}, u32[]{:S(2)}) %all-to-all-start) | async-done | bytes 262176 | tf_op jit(solution)/shard_map/all_to_all | solution.py:282
  38.3 7.7 %collective-permute-start.1 = (bf16[512,256]{1,0:T(8,128)(2,1)S(1)}, bf16[512,256]{1,0:T(8,128)(2,1)S(1)}, u32[]{:S(2)}, u32[]{:S(2)}) collective-permute-start(bf16[512,256]{1,0:T(8,128)(2,1)S(1)} %bitcast.7), channel_id=1, source_target_pairs={{0,512},{64,576},{128,640},{192,704},{256,768},{320,832},{384,896}... | collective-permute-start | bytes 786440 | tf_op jit(solution)/shard_map/ppermute | solution.py:289
  46.0 0.0 collective-permute-done.pack_ref
  46.1 0.9 %shard_map.70 = (bf16[512,512]{1,0:T(8,128)(2,1)S(1)}, bf16[256,256]{1,0:T(8,128)(2,1)S(1)}, f32[512,256]{1,0:T(8,128)S(1)}) custom-call(bf16[512,512]{1,0:T(8,128)(2,1)S(1)} %get-tuple-element.14.root_ref, bf16[528,256]{1,0:T(8,128)(2,1)S(1)} %collective-permute-done.pack_ref, bf16[512,256]{1,0:T(8,128)(2,1)S(1)} %bitcast.8), custom_call_target="tpu_custom_call" | custom-call | flops 536870912 | bytes 1835008 | tf_op jit(solution)/shard_map/pallas_call | solution.py:198
  47.0 8.4 %collective-permute-done.1.other_ref = bf16[512,256]{1,0:T(8,128)(2,1)S(1)} collective-permute-done((bf16[512,256]{1,0:T(8,128)(2,1)S(1)}, bf16[512,256]{1,0:T(8,128)(2,1)S(1)}, u32[]{:S(2)}, u32[]{:S(2)}) %collective-permute-start.1) | collective-permute-done | bytes 262176 | tf_op jit(solution)/shard_map/ppermute | solution.py:289
  55.4 0.0 copy-start.1
  55.4 1.2 %shard_map.71 = bf16[512,256]{1,0:T(8,128)(2,1)} custom-call(bf16[512,512]{1,0:T(8,128)(2,1)S(1)} %get-tuple-element.18.left_ref, bf16[256,256]{1,0:T(8,128)(2,1)S(1)} %get-tuple-element.19.right_ref, f32[512,256]{1,0:T(8,128)S(1)} %get-tuple-element.20.total_ref, bf16[512,256]{1,0:T(8,128)(2,1)S(1)} %collective-permute-done.1.other_ref), custom_call_target="tpu_custom_call" | custom-call | flops 268435456 | bytes 1572864 | tf_op jit(solution)/shard_map/pallas_call | solution.py:220
  56.6 11.5 %all-to-all-start.1 = ((bf16[16,32,256]{2,1,0:T(8,128)(2,1)}), bf16[16,32,256]{2,1,0:T(8,128)(2,1)S(1)}, u32[]{:S(2)}, u32[]{:S(2)}) async-start(bf16[16,32,256]{2,1,0:T(8,128)(2,1)} %bitcast.4), calls=%async_computation.1 | async-start | bytes 524288 | tf_op jit(solution)/shard_map/all_to_all | solution.py:293
  68.1 0.0 copy-done.1
  68.1 1.5 %shard_map.73 = f32[512,512]{1,0:T(8,128)} custom-call(f32[512,512]{1,0:T(8,128)S(1)} %bitcast.11, bf16[512,256]{1,0:T(8,128)(2,1)S(1)} %bitcast.9, bf16[512,256]{1,0:T(8,128)(2,1)S(1)} %collective-permute-done.1.other_ref), custom_call_target="tpu_custom_call" | custom-call | flops 268435456 | bytes 2621440 | tf_op jit(solution)/shard_map/pallas_call | solution.py:262
  69.6 16.9 %all-to-all-done.1.got_ref = bf16[16,32,256]{2,1,0:T(8,128)(2,1)S(1)} async-done(((bf16[16,32,256]{2,1,0:T(8,128)(2,1)}), bf16[16,32,256]{2,1,0:T(8,128)(2,1)S(1)}, u32[]{:S(2)}, u32[]{:S(2)}) %all-to-all-start.1) | async-done | bytes 262176 | tf_op jit(solution)/shard_map/all_to_all | solution.py:293
  86.4 0.8 shard_map.72
Async XLA Ops:
  0.6 23.4 %copy-start.2 = (bf16[1,1,1,512,512]{4,3,2,1,0:T(8,128)(2,1)S(1)}, bf16[1,1,1,512,512]{4,3,2,1,0:T(8,128)(2,1)}, u32[]{:S(2)}) copy-start(bf16[1,1,1,512,512]{4,3,2,1,0:T(8,128)(2,1)} %param.9) | copy-start | bytes 1572868
  2.5 35.8 %all-to-all-start = ((bf16[16,32,256]{2,1,0:T(8,128)(2,1)}), bf16[16,32,256]{2,1,0:T(8,128)(2,1)S(1)}, u32[]{:S(2)}, u32[]{:S(2)}) async-start(bf16[16,32,256]{2,1,0:T(8,128)(2,1)} %get-tuple-element.16), calls=%async_computation | async-start | bytes 524288 | tf_op jit(solution)/shard_map/all_to_all | solution.py:282
  24.0 1.2 %copy-start = (f32[1,1,1,512,512]{4,3,2,1,0:T(8,128)S(1)}, f32[1,1,1,512,512]{4,3,2,1,0:T(8,128)}, u32[]{:S(2)}) copy-start(f32[1,1,1,512,512]{4,3,2,1,0:T(8,128)} %param.8) | copy-start | bytes 3145732
  27.0 19.1 %collective-permute-start = (bf16[528,256]{1,0:T(8,128)(2,1)S(1)}, bf16[528,256]{1,0:T(8,128)(2,1)S(1)}, u32[]{:S(2)}, u32[]{:S(2)}) collective-permute-start(bf16[528,256]{1,0:T(8,128)(2,1)S(1)} %get-tuple-element.15), channel_id=1, source_target_pairs={{0,512},{64,576},{128,640},{192,704},{256,768},{320,832},{384,896}... | collective-permute-start | bytes 811016 | tf_op jit(solution)/shard_map/ppermute | solution.py:287
  38.3 17.1 %collective-permute-start.1 = (bf16[512,256]{1,0:T(8,128)(2,1)S(1)}, bf16[512,256]{1,0:T(8,128)(2,1)S(1)}, u32[]{:S(2)}, u32[]{:S(2)}) collective-permute-start(bf16[512,256]{1,0:T(8,128)(2,1)S(1)} %bitcast.7), channel_id=1, source_target_pairs={{0,512},{64,576},{128,640},{192,704},{256,768},{320,832},{384,896}... | collective-permute-start | bytes 786440 | tf_op jit(solution)/shard_map/ppermute | solution.py:289
  55.4 12.7 %copy-start.1 = (f32[1,1,1,512,512]{4,3,2,1,0:T(8,128)S(1)}, f32[1,1,1,512,512]{4,3,2,1,0:T(8,128)}, u32[]{:S(2)}) copy-start(f32[1,1,1,512,512]{4,3,2,1,0:T(8,128)} %param.8) | copy-start | bytes 3145732
  56.6 29.8 %all-to-all-start.1 = ((bf16[16,32,256]{2,1,0:T(8,128)(2,1)}), bf16[16,32,256]{2,1,0:T(8,128)(2,1)S(1)}, u32[]{:S(2)}, u32[]{:S(2)}) async-start(bf16[16,32,256]{2,1,0:T(8,128)(2,1)} %bitcast.4), calls=%async_computation.1 | async-start | bytes 524288 | tf_op jit(solution)/shard_map/all_to_all | solution.py:293
